TPU v7x, 256 devices: a whole 4x4x8 slice. The times are simulated.
256 devices in a mesh: dom: 64 (over z, y, core), rel: 4 (over x).
Axes of the slice: x: 4, y: 4, z: 8, core: 2. Of those that a mesh axis runs over, the one named last changes fastest.
Arguments:
- embeddings: float32 [131072, 400], P('dom'), may hold values from -3 to 3
- rel_weight: float32 [256, 400], P('rel'), may hold values from -4 to 4
- head_row: int32 [98304], P(('dom', 'rel')), may hold values from 0 to 2047
- rel_id: int32 [98304], P(('dom', 'rel')), may hold values from 0 to 63
- tail_owner: int32 [98304, 1], P(('dom', 'rel')), may hold values from 0 to 63; in each aligned block of 384 rows (0 to 383, 384 to 767, ...) at most 12 rows name the same one
- tail_row: int32 [98304], P(('dom', 'rel')), may hold values from 0 to 2047
- neg_owner: int32 [24576, 1], P('dom'), may hold values from 0 to 63; in each aligned block of 96 rows (0 to 95, 96 to 191, ...) at most 3 rows name the same one
- neg_row: int32 [24576], P('dom'), may hold values from 0 to 2047
Outputs:
- embedding_grad: float32 [131072, 400], P('dom')
- relation_grad: float32 [256, 400], P('rel')
Inputs may be any that keep to these rules, and one draw needn't show every extreme that they name: `tail_owner`: in the rows of one device no partition is named more than 12 times, and it is reached. `neg_owner`: in each aligned block of 96 rows no partition is named more than 3 times, and it is reached.
All inputs are finite; a program needn't handle non-finite values.
Results may differ from a plain program's by a relative error of at most 0.0003.
Values sent between devices are 32-bit elements; how exact they have to be, the bound alone decides.
A program may use at most 64 MiB of HBM per device.

v0:
```python
import jax
import jax.numpy as jnp
from jax import lax
from jax.sharding import PartitionSpec as P

SPAN = 128
NEG = 128


def span_grads(head_emb, rel_rows, tail_emb, neg_emb):
    queries = head_emb * rel_rows
    positive = jnp.sum(queries * tail_emb, axis=1)
    scores = jnp.dot(queries, neg_emb.T, precision=lax.Precision.HIGHEST)
    row_max = jnp.maximum(positive, jnp.max(scores, axis=1))
    pos_exp = jnp.exp(positive - row_max)
    neg_exp = jnp.exp(scores - row_max[:, None])
    total = pos_exp + jnp.sum(neg_exp, axis=1)
    pos_coef = pos_exp / total - 1.0
    neg_coef = neg_exp / total[:, None]
    grad_query = pos_coef[:, None] * tail_emb + jnp.dot(
        neg_coef, neg_emb, precision=lax.Precision.HIGHEST
    )
    grad_tail = pos_coef[:, None] * queries
    grad_neg = jnp.dot(neg_coef.T, queries, precision=lax.Precision.HIGHEST)
    return (grad_query * rel_rows, grad_query * head_emb, grad_tail, grad_neg)


def slot_of(owner, dom_count, capacity):
    onehot = (owner[:, None] == jnp.arange(dom_count, dtype=jnp.int32)[None, :]).astype(jnp.int32)
    position = jnp.sum((jnp.cumsum(onehot, axis=0) - 1) * onehot, axis=1)
    return owner * capacity + position


def id_buffer(slot_index, rows, dom_count, capacity):
    filled = jnp.zeros((dom_count * capacity,), jnp.int32).at[slot_index].set(rows)
    return filled.reshape(dom_count, capacity)


def grad_buffer(slot_index, values, dom_count, capacity):
    filled = (
        jnp.zeros((dom_count * capacity, values.shape[1]), jnp.float32).at[slot_index].set(values)
    )
    return filled.reshape(dom_count, capacity, values.shape[1])


def serve(embeddings, asked):
    width = embeddings.shape[1]
    return embeddings[asked.reshape(-1)].reshape(asked.shape[0], asked.shape[1], width)


def body(embeddings, rel_weight, head_row, rel_id, tail_owner, tail_row, neg_owner, neg_row):
    dom_count = lax.axis_size("dom")
    rel_count = lax.axis_size("rel")
    width = embeddings.shape[1]
    edges = head_row.shape[0]
    neg_total = neg_row.shape[0]
    spans = edges // SPAN
    part_len = neg_total // rel_count
    tail_cap = 2 * edges // dom_count
    part_cap = 2 * part_len // dom_count
    tail_slot = slot_of(tail_owner[:, 0], dom_count, tail_cap)
    tail_ids = id_buffer(tail_slot, tail_row, dom_count, tail_cap)
    neg_cap = rel_count * part_cap
    neg_slot = slot_of(neg_owner[:, 0], dom_count, neg_cap)
    neg_ids = id_buffer(neg_slot, neg_row, dom_count, neg_cap)
    asked_tail, asked_neg = (
        lax.all_to_all(tail_ids, "dom", split_axis=0, concat_axis=0, tiled=True),
        lax.all_to_all(neg_ids, "dom", split_axis=0, concat_axis=0, tiled=True),
    )
    got_tail, got_neg = (
        lax.all_to_all(
            serve(embeddings, asked_tail), "dom", split_axis=0, concat_axis=0, tiled=True
        ),
        lax.all_to_all(
            serve(embeddings, asked_neg), "dom", split_axis=0, concat_axis=0, tiled=True
        ),
    )
    neg_emb = got_neg.reshape(-1, width)[neg_slot]
    tail_emb = got_tail.reshape(-1, width)[tail_slot]
    head_emb = embeddings[head_row]
    rel_rows = rel_weight[rel_id]
    grad_head, grad_rel, grad_tail, grad_neg = jax.vmap(span_grads)(
        head_emb.reshape(spans, SPAN, width),
        rel_rows.reshape(spans, SPAN, width),
        tail_emb.reshape(spans, SPAN, width),
        neg_emb.reshape(spans, NEG, width),
    )
    slab_grad = (
        jnp.zeros(embeddings.shape, jnp.float32).at[head_row].add(grad_head.reshape(-1, width))
    )
    rel_local = jnp.zeros(rel_weight.shape, jnp.float32).at[rel_id].add(grad_rel.reshape(-1, width))
    tail_back = grad_buffer(tail_slot, grad_tail.reshape(-1, width), dom_count, tail_cap)
    neg_back = grad_buffer(neg_slot, grad_neg.reshape(-1, width), dom_count, rel_count * part_cap)
    recv_tail, recv_neg = (
        lax.all_to_all(tail_back, "dom", split_axis=0, concat_axis=0, tiled=True),
        lax.all_to_all(neg_back, "dom", split_axis=0, concat_axis=0, tiled=True),
    )
    slab_grad = slab_grad.at[asked_tail.reshape(-1)].add(recv_tail.reshape(-1, width))
    slab_grad = slab_grad.at[asked_neg.reshape(-1)].add(recv_neg.reshape(-1, width))
    embedding_grad = lax.psum(slab_grad, "rel")
    relation_grad = lax.psum(rel_local, "dom")
    return (embedding_grad, relation_grad)


def solution(mesh):
    return jax.shard_map(
        body,
        mesh=mesh,
        in_specs=(
            P("dom", None),
            P("rel", None),
            P(("dom", "rel")),
            P(("dom", "rel")),
            P(("dom", "rel"), None),
            P(("dom", "rel")),
            P("dom", None),
            P("dom"),
        ),
        out_specs=(P("dom", None), P("rel", None)),
        check_vma=False,
    )
```

profile of v0, /device:TPU:1, one launch (start us, length us, event | category | flops | bytes accessed | tf_op | source)
XLA Modules:
  0.0 593.7 jit_solution(2802582018687139575)
XLA Ops:
  9.9 3.1 scatter_custom_fusion
  13.7 13.2 %all-to-all-start = ((s32[64,1,12]{2,1,0:T(1,128)}), s32[64,1,12]{2,1,0:T(1,128)S(1)}, u32[]{:S(2)}, u32[]{:S(2)}) async-start(s32[64,1,12]{2,1,0:T(1,128)} %bitcast.1), calls=%async_computation | async-start | bytes 65536 | tf_op jit(solution)/shard_map/all_to_all | solution.py:67
  29.6 5.0 copy.41
  34.6 3.1 scatter_custom_fusion.1
  38.4 10.3 %all-to-all-start.2 = ((s32[64,1,12]{2,1,0:T(1,128)}), s32[64,1,12]{2,1,0:T(1,128)S(1)}, u32[]{:S(2)}, u32[]{:S(2)}) async-start(s32[64,1,12]{2,1,0:T(1,128)} %bitcast.6), calls=%async_computation.2 | async-start | bytes 65536 | tf_op jit(solution)/shard_map/all_to_all | solution.py:68
  50.1 5.0 gather_fusion.2
  58.0 8.9 %all-to-all-start.1 = ((f32[64,12,400]{2,1,0:T(8,128)}), f32[64,12,400]{2,1,0:T(8,128)S(1)}, u32[]{:S(2)}, u32[]{:S(2)}) async-start(f32[64,12,400]{2,1,0:T(8,128)} %reshape.203), calls=%async_computation.1 | async-start | bytes 4194304 | tf_op jit(solution)/shard_map/all_to_all | solution.py:71
  67.8 5.7 gather_fusion.4
  76.1 40.5 %all-to-all-done.1 = f32[64,12,400]{2,1,0:T(8,128)S(1)} async-done(((f32[64,12,400]{2,1,0:T(8,128)}), f32[64,12,400]{2,1,0:T(8,128)S(1)}, u32[]{:S(2)}, u32[]{:S(2)}) %all-to-all-start.1) | async-done | bytes 1228832 | tf_op jit(solution)/shard_map/all_to_all | solution.py:71
  117.9 7.6 %all-to-all-start.3 = ((f32[64,12,400]{2,1,0:T(8,128)}), f32[64,12,400]{2,1,0:T(8,128)}, u32[]{:S(2)}, u32[]{:S(2)}) async-start(f32[64,12,400]{2,1,0:T(8,128)} %reshape.209), calls=%async_computation.3 | async-start | bytes 4194304 | tf_op jit(solution)/shard_map/all_to_all | solution.py:74
  125.6 4.2 gather_fusion
  139.7 35.2 %all-to-all-done.3 = f32[64,12,400]{2,1,0:T(8,128)} async-done(((f32[64,12,400]{2,1,0:T(8,128)}), f32[64,12,400]{2,1,0:T(8,128)}, u32[]{:S(2)}, u32[]{:S(2)}) %all-to-all-start.3) | async-done | bytes 1228832 | tf_op jit(solution)/shard_map/all_to_all | solution.py:74
  185.6 7.4 %all-to-all-start.4 = ((f32[64,12,400]{2,1,0:T(8,128)}), f32[64,12,400]{2,1,0:T(8,128)}, u32[]{:S(2)}, u32[]{:S(2)}) async-start(f32[64,12,400]{2,1,0:T(8,128)} %reshape.214), calls=%async_computation.4 | async-start | bytes 4194304 | tf_op jit(solution)/shard_map/all_to_all | solution.py:95
  199.2 43.4 %all-to-all-done.4 = f32[64,12,400]{2,1,0:T(8,128)} async-done(((f32[64,12,400]{2,1,0:T(8,128)}), f32[64,12,400]{2,1,0:T(8,128)}, u32[]{:S(2)}, u32[]{:S(2)}) %all-to-all-start.4) | async-done | bytes 1228832 | tf_op jit(solution)/shard_map/all_to_all | solution.py:95
  242.6 7.2 %all-to-all-start.5 = ((f32[64,12,400]{2,1,0:T(8,128)}), f32[64,12,400]{2,1,0:T(8,128)}, u32[]{:S(2)}, u32[]{:S(2)}) async-start(f32[64,12,400]{2,1,0:T(8,128)} %reshape.217), calls=%async_computation.5 | async-start | bytes 4194304 | tf_op jit(solution)/shard_map/all_to_all | solution.py:96
  252.8 3.3 fusion.36
  257.4 5.0 scatter_custom_fusion.2
  264.1 10.7 %scatter_fusion = f32[2048,400]{1,0:T(8,128)} fusion(f32[2048,400]{1,0:T(8,128)} %scatter_custom_fusion.2, s32[768]{0:T(1024)S(1)} %fusion.24, f32[768,400]{1,0:T(8,128)S(1)} %reshape.304), kind=kCustom, calls=%fused_computation.10 | custom fusion | flops 307200 | bytes 3689472 | tf_op jit(solution)/shard_map/scatter-add | solution.py:98
  274.7 24.6 %all-to-all-done.5 = f32[64,12,400]{2,1,0:T(8,128)} async-done(((f32[64,12,400]{2,1,0:T(8,128)}), f32[64,12,400]{2,1,0:T(8,128)}, u32[]{:S(2)}, u32[]{:S(2)}) %all-to-all-start.5) | async-done | bytes 1228832 | tf_op jit(solution)/shard_map/all_to_all | solution.py:96
  301.0 10.7 %scatter_fusion.1 = f32[2048,400]{1,0:T(8,128)} fusion(f32[2048,400]{1,0:T(8,128)} %scatter_fusion, s32[768]{0:T(1024)S(1)} %fusion.25, f32[768,400]{1,0:T(8,128)S(1)} %reshape.320), kind=kCustom, calls=%fused_computation.12 | custom fusion | flops 307200 | bytes 3689472 | tf_op jit(solution)/shard_map/scatter-add | solution.py:99
  312.2 3.4 scatter_custom_fusion.7
  315.7 91.7 %all-reduce.3.cloned.1.call-done = f32[2048,400]{1,0:T(8,128)} async-done(((f32[2048,400]{1,0:T(8,128)}), f32[2048,400]{1,0:T(8,128)}) %all-reduce.3.cloned.1.call-update) | async-done | bytes 3276816 | tf_op jit(solution)/shard_map/psum | solution.py:100
  407.4 5.2 copy.66
  412.6 172.5 %all-reduce.5.cloned.1.call-done = f32[64,400]{1,0:T(8,128)} async-done(((f32[64,400]{1,0:T(8,128)}), f32[64,400]{1,0:T(8,128)}) %all-reduce.5.cloned.1.call-update) | async-done | bytes 102416 | tf_op jit(solution)/shard_map/psum | solution.py:101
  (82 shorter events, 52.3 us)
Async XLA Ops:
  7.2 123.4 %copy-start = (f32[64,400]{1,0:T(8,128)S(1)}, f32[64,400]{1,0:T(8,128)}, u32[]{:S(2)}) copy-start(f32[64,400]{1,0:T(8,128)} %param.9) | copy-start | bytes 307204
  13.7 24.7 %all-to-all-start = ((s32[64,1,12]{2,1,0:T(1,128)}), s32[64,1,12]{2,1,0:T(1,128)S(1)}, u32[]{:S(2)}, u32[]{:S(2)}) async-start(s32[64,1,12]{2,1,0:T(1,128)} %bitcast.1), calls=%async_computation | async-start | bytes 65536 | tf_op jit(solution)/shard_map/all_to_all | solution.py:67
  38.4 19.6 %all-to-all-start.2 = ((s32[64,1,12]{2,1,0:T(1,128)}), s32[64,1,12]{2,1,0:T(1,128)S(1)}, u32[]{:S(2)}, u32[]{:S(2)}) async-start(s32[64,1,12]{2,1,0:T(1,128)} %bitcast.6), calls=%async_computation.2 | async-start | bytes 65536 | tf_op jit(solution)/shard_map/all_to_all | solution.py:68
  58.0 58.6 %all-to-all-start.1 = ((f32[64,12,400]{2,1,0:T(8,128)}), f32[64,12,400]{2,1,0:T(8,128)S(1)}, u32[]{:S(2)}, u32[]{:S(2)}) async-start(f32[64,12,400]{2,1,0:T(8,128)} %reshape.203), calls=%async_computation.1 | async-start | bytes 4194304 | tf_op jit(solution)/shard_map/all_to_all | solution.py:71
  76.1 49.5 %copy-start.6 = (s32[384]{0:T(512)S(1)}, s32[384]{0:T(512)}, u32[]{:S(2)}) copy-start(s32[384]{0:T(512)} %param.10) | copy-start | bytes 4612
  116.6 1.3 copy-start.1
  117.9 57.0 %all-to-all-start.3 = ((f32[64,12,400]{2,1,0:T(8,128)}), f32[64,12,400]{2,1,0:T(8,128)}, u32[]{:S(2)}, u32[]{:S(2)}) async-start(f32[64,12,400]{2,1,0:T(8,128)} %reshape.209), calls=%async_computation.3 | async-start | bytes 4194304 | tf_op jit(solution)/shard_map/all_to_all | solution.py:74
  129.8 0.7 copy-start.7
  185.6 7.4 %copy-start.4 = (f32[3,128,400]{1,0,2:T(4,128)S(1)}, f32[3,128,400]{1,0,2:T(4,128)}, u32[]{:S(2)}) copy-start(f32[3,128,400]{1,0,2:T(4,128)} %mul.52) | copy-start | bytes 1843204
  185.6 57.0 %all-to-all-start.4 = ((f32[64,12,400]{2,1,0:T(8,128)}), f32[64,12,400]{2,1,0:T(8,128)}, u32[]{:S(2)}, u32[]{:S(2)}) async-start(f32[64,12,400]{2,1,0:T(8,128)} %reshape.214), calls=%async_computation.4 | async-start | bytes 4194304 | tf_op jit(solution)/shard_map/all_to_all | solution.py:95
  242.6 56.8 %all-to-all-start.5 = ((f32[64,12,400]{2,1,0:T(8,128)}), f32[64,12,400]{2,1,0:T(8,128)}, u32[]{:S(2)}, u32[]{:S(2)}) async-start(f32[64,12,400]{2,1,0:T(8,128)} %reshape.217), calls=%async_computation.5 | async-start | bytes 4194304 | tf_op jit(solution)/shard_map/all_to_all | solution.py:96
  249.8 1.9 copy-start.3
  249.8 157.6 %all-reduce.3.cloned.1.call-start = ((), (), s32[]{:S(2)}) async-start(), calls=%async_computation.6 | async-start | bytes 8388608 | tf_op jit(solution)/shard_map/psum | solution.py:100
  250.6 2.2 copy-start.2
  251.7 1.1 copy-start.5
  311.7 273.4 %all-reduce.5.cloned.1.call-start = ((), (), s32[]{:S(2)}) async-start(), calls=%async_computation.7 | async-start | bytes 262144 | tf_op jit(solution)/shard_map/psum | solution.py:101
Sparse Core Ops, SparseCore 0:
  311.8 95.5 all-reduce.2
  411.9 173.2 all-reduce.4
where the time goes:
time: 602 us; the launch traced here: 594 us
  waiting for transfers between devices  409 us (68%)
  local copies, waits for them, and re-layouts  64.5 us (11%)
  starting transfers between devices  55.3 us (9%)
  other arithmetic  42.6 us (7%)
  between operations  14.6 us (2%)
  matrix products  7.26 us (1%)
    psum x1, waiting for transfers between devices, body(): relation_grad = lax.psum(rel_local, 'dom')  173 us
    psum x1, waiting for transfers between devices, body(): embedding_grad = lax.psum(slab_grad, 'rel')  91.7 us
    all_to_all x1, waiting for transfers between devices, body(): lax.all_to_all(tail_back, 'dom', split_axis=0, concat_axis=0, tiled=True)  43.4 us
    all_to_all x1, waiting for transfers between devices, body(): lax.all_to_all(serve(embeddings, asked_tail), 'dom', split_axis=0, concat...  40.5 us
    all_to_all x1, waiting for transfers between devices, body(): lax.all_to_all(serve(embeddings, asked_neg), 'dom', split_axis=0, concat_...  35.2 us
    all_to_all x1, waiting for transfers between devices, body(): lax.all_to_all(neg_back, 'dom', split_axis=0, concat_axis=0, tiled=True)  24.6 us
    unnamed x19, local copies, waits for them, and re-layouts  13.4 us
    all_to_all x1, starting transfers between devices, body(): lax.all_to_all(tail_ids, 'dom', split_axis=0, concat_axis=0, tiled=True)  13.2 us
  transfers between devices with their start and end apart: 8, of which 7 were waited for; matrix products, arithmetic and copies ran while one was open for 14% of the time, Pallas kernels for 0%

commit v1 on v0

--- a/solution.py
+++ b/solution.py
@@ -97,7 +97,7 @@
     )
     slab_grad = slab_grad.at[asked_tail.reshape(-1)].add(recv_tail.reshape(-1, width))
     slab_grad = slab_grad.at[asked_neg.reshape(-1)].add(recv_neg.reshape(-1, width))
-    embedding_grad = lax.psum(slab_grad, "rel")
+    embedding_grad = jnp.sum(lax.all_gather(slab_grad, "rel"), axis=0)
     relation_grad = lax.psum(rel_local, "dom")
     return (embedding_grad, relation_grad)
 

time: 602 us -> 508 us (0.84)
  waiting for transfers between devices: 409 us -> 302 us
  other arithmetic: 42.6 us -> 54.1 us
    psum x1, waiting for transfers between devices: 173 us -> 7.26 us  [body(): relation_grad = lax.psum(rel_local, 'dom')]
    all_gather x0 -> x1, waiting for transfers between devices: none -> 150 us  [body(): embedding_grad = jnp.sum(lax.all_gather(slab_grad, 'rel'), axis=0)]
    psum x1 -> x0, waiting for transfers between devices: 91.7 us -> none  [body(): embedding_grad = lax.psum(slab_grad, 'rel')]
    reduce_sum x0 -> x1, other arithmetic: none -> 10.5 us  [body(): embedding_grad = jnp.sum(lax.all_gather(slab_grad, 'rel'), axis=0)]
    unnamed x19 -> x21, local copies, waits for them, and re-layouts: 13.4 us -> 13.4 us
  transfers between devices with their start and end apart: 8 -> 8, of which waited for: 7 -> 7; matrix products, arithmetic and copies ran while one was open for 14% -> 19% of each run, Pallas kernels for 0% -> 0%
where the time goes in v1:
time: 508 us; the launch traced here: 499 us
  waiting for transfers between devices  302 us (59%)
  local copies, waits for them, and re-layouts  65.2 us (13%)
  starting transfers between devices  55.3 us (11%)
  other arithmetic  54.1 us (11%)
  between operations  16 us (3%)
  matrix products  6.64 us (1%)
    all_gather x1, waiting for transfers between devices, body(): embedding_grad = jnp.sum(lax.all_gather(slab_grad, 'rel'), axis=0)  150 us
    all_to_all x1, waiting for transfers between devices, body(): lax.all_to_all(tail_back, 'dom', split_axis=0, concat_axis=0, tiled=True)  43.5 us
    all_to_all x1, waiting for transfers between devices, body(): lax.all_to_all(serve(embeddings, asked_tail), 'dom', split_axis=0, concat...  40.5 us
    all_to_all x1, waiting for transfers between devices, body(): lax.all_to_all(serve(embeddings, asked_neg), 'dom', split_axis=0, concat_...  33.2 us
    all_to_all x1, waiting for transfers between devices, body(): lax.all_to_all(neg_back, 'dom', split_axis=0, concat_axis=0, tiled=True)  25.8 us
    unnamed x21, local copies, waits for them, and re-layouts  13.4 us
    all_to_all x1, starting transfers between devices, body(): lax.all_to_all(tail_ids, 'dom', split_axis=0, concat_axis=0, tiled=True)  13.2 us
    gather x2, local copies, waits for them, and re-layouts, serve(): embeddings[asked.reshape(-1)].reshape(asked.shape[0], asked.shape[1], width)  10.6 us
  transfers between devices with their start and end apart: 8, of which 7 were waited for; matrix products, arithmetic and copies ran while one was open for 19% of the time, Pallas kernels for 0%

profile of v1, /device:TPU:1, one launch (start us, length us, event | category | flops | bytes accessed | tf_op | source)
XLA Modules:
  0.0 499.3 jit_solution(16906456426211479892)
XLA Ops:
  10.8 3.1 scatter_custom_fusion
  14.6 13.2 %all-to-all-start = ((s32[64,1,12]{2,1,0:T(1,128)}), s32[64,1,12]{2,1,0:T(1,128)S(1)}, u32[]{:S(2)}, u32[]{:S(2)}) async-start(s32[64,1,12]{2,1,0:T(1,128)} %bitcast.1), calls=%async_computation | async-start | bytes 65536 | tf_op jit(solution)/shard_map/all_to_all | solution.py:67
  30.4 3.1 scatter_custom_fusion.1
  34.2 5.0 copy.61
  39.2 10.3 %all-to-all-start.2 = ((s32[64,1,12]{2,1,0:T(1,128)}), s32[64,1,12]{2,1,0:T(1,128)S(1)}, u32[]{:S(2)}, u32[]{:S(2)}) async-start(s32[64,1,12]{2,1,0:T(1,128)} %bitcast.6), calls=%async_computation.2 | async-start | bytes 65536 | tf_op jit(solution)/shard_map/all_to_all | solution.py:68
  50.9 5.0 gather_fusion.2
  58.8 8.9 %all-to-all-start.1 = ((f32[64,12,400]{2,1,0:T(8,128)}), f32[64,12,400]{2,1,0:T(8,128)S(1)}, u32[]{:S(2)}, u32[]{:S(2)}) async-start(f32[64,12,400]{2,1,0:T(8,128)} %reshape.203), calls=%async_computation.1 | async-start | bytes 4194304 | tf_op jit(solution)/shard_map/all_to_all | solution.py:71
  68.6 5.7 %gather_fusion.4 = f32[768,400]{1,0:T(8,128)} fusion(f32[2048,400]{1,0:T(8,128)} %copy.61, s32[1024]{0:T(1024)S(1)} %pad_clamp_fusion.1), kind=kCustom, calls=%fused_computation.4 | custom fusion | bytes 2460672 | tf_op jit(solution)/shard_map/gather | solution.py:48
  76.9 40.5 %all-to-all-done.1 = f32[64,12,400]{2,1,0:T(8,128)S(1)} async-done(((f32[64,12,400]{2,1,0:T(8,128)}), f32[64,12,400]{2,1,0:T(8,128)S(1)}, u32[]{:S(2)}, u32[]{:S(2)}) %all-to-all-start.1) | async-done | bytes 1228832 | tf_op jit(solution)/shard_map/all_to_all | solution.py:71
  118.8 7.9 %all-to-all-start.3 = ((f32[64,12,400]{2,1,0:T(8,128)}), f32[64,12,400]{2,1,0:T(8,128)}, u32[]{:S(2)}, u32[]{:S(2)}) async-start(f32[64,12,400]{2,1,0:T(8,128)} %reshape.209), calls=%async_computation.3 | async-start | bytes 4194304 | tf_op jit(solution)/shard_map/all_to_all | solution.py:74
  129.0 4.2 gather_fusion
  142.8 33.2 %all-to-all-done.3 = f32[64,12,400]{2,1,0:T(8,128)} async-done(((f32[64,12,400]{2,1,0:T(8,128)}), f32[64,12,400]{2,1,0:T(8,128)}, u32[]{:S(2)}, u32[]{:S(2)}) %all-to-all-start.3) | async-done | bytes 1228832 | tf_op jit(solution)/shard_map/all_to_all | solution.py:74
  186.6 7.4 %all-to-all-start.4 = ((f32[64,12,400]{2,1,0:T(8,128)}), f32[64,12,400]{2,1,0:T(8,128)}, u32[]{:S(2)}, u32[]{:S(2)}) async-start(f32[64,12,400]{2,1,0:T(8,128)} %reshape.214), calls=%async_computation.4 | async-start | bytes 4194304 | tf_op jit(solution)/shard_map/all_to_all | solution.py:95
  200.1 43.5 %all-to-all-done.4 = f32[64,12,400]{2,1,0:T(8,128)} async-done(((f32[64,12,400]{2,1,0:T(8,128)}), f32[64,12,400]{2,1,0:T(8,128)}, u32[]{:S(2)}, u32[]{:S(2)}) %all-to-all-start.4) | async-done | bytes 1228832 | tf_op jit(solution)/shard_map/all_to_all | solution.py:95
  243.6 7.2 %all-to-all-start.5 = ((f32[64,12,400]{2,1,0:T(8,128)}), f32[64,12,400]{2,1,0:T(8,128)}, u32[]{:S(2)}, u32[]{:S(2)}) async-start(f32[64,12,400]{2,1,0:T(8,128)} %reshape.217), calls=%async_computation.5 | async-start | bytes 4194304 | tf_op jit(solution)/shard_map/all_to_all | solution.py:96
  257.3 5.0 scatter_custom_fusion.2
  263.9 10.6 %scatter_fusion = f32[2048,400]{1,0:T(8,128)} fusion(f32[2048,400]{1,0:T(8,128)} %scatter_custom_fusion.2, s32[768]{0:T(1024)S(1)} %fusion.24, f32[768,400]{1,0:T(8,128)S(1)} %reshape.304), kind=kCustom, calls=%fused_computation.10 | custom fusion | flops 307200 | bytes 3689472 | tf_op jit(solution)/shard_map/scatter-add | solution.py:98
  274.6 25.8 %all-to-all-done.5 = f32[64,12,400]{2,1,0:T(8,128)} async-done(((f32[64,12,400]{2,1,0:T(8,128)}), f32[64,12,400]{2,1,0:T(8,128)}, u32[]{:S(2)}, u32[]{:S(2)}) %all-to-all-start.5) | async-done | bytes 1228832 | tf_op jit(solution)/shard_map/all_to_all | solution.py:96
  302.0 10.6 %scatter_fusion.1 = f32[2048,400]{1,0:T(8,128)} fusion(f32[2048,400]{1,0:T(8,128)} %scatter_fusion, s32[768]{0:T(1024)S(1)} %fusion.25, f32[768,400]{1,0:T(8,128)S(1)} %reshape.320), kind=kCustom, calls=%fused_computation.12 | custom fusion | flops 307200 | bytes 3689472 | tf_op jit(solution)/shard_map/scatter-add | solution.py:99
  313.2 3.4 scatter_custom_fusion.7
  316.7 150.4 %all-gather.3.cloned.1.call-done = f32[8192,400]{1,0:T(8,128)} async-done(((f32[2048,400]{1,0:T(8,128)}), f32[8192,400]{1,0:T(8,128)}) %all-gather.3.cloned.1.call-update) | async-done | bytes 13107216 | tf_op jit(solution)/shard_map/all_gather | solution.py:100
  467.2 10.5 %reduce_sum.61 = f32[2048,400]{1,0:T(8,128)} reduce(f32[4,2048,400]{2,1,0:T(8,128)} %bitcast.73, f32[]{:T(128)} %constant.9.clone.1), dimensions={0}, to_apply=%region_16.17 | reduce | flops 2457600 | bytes 16384004 | tf_op jit(solution)/shard_map/reduce_sum | solution.py:100
  477.6 5.2 %copy.86 = f32[2048,400]{0,1:T(8,128)} copy(f32[2048,400]{1,0:T(8,128)} %reduce_sum.61) | data formatting | bytes 6553600
  482.8 7.3 %all-reduce.2.cloned.1.call-done = f32[64,400]{1,0:T(8,128)} async-done(((f32[64,400]{1,0:T(8,128)}), f32[64,400]{1,0:T(8,128)}) %all-reduce.2.cloned.1.call-update) | async-done | bytes 102416 | tf_op jit(solution)/shard_map/psum | solution.py:101
  (85 shorter events, 56.5 us)
Async XLA Ops:
  8.0 118.7 %copy-start = (f32[64,400]{1,0:T(8,128)S(1)}, f32[64,400]{1,0:T(8,128)}, u32[]{:S(2)}) copy-start(f32[64,400]{1,0:T(8,128)} %param.9) | copy-start | bytes 307204
  14.6 24.7 %all-to-all-start = ((s32[64,1,12]{2,1,0:T(1,128)}), s32[64,1,12]{2,1,0:T(1,128)S(1)}, u32[]{:S(2)}, u32[]{:S(2)}) async-start(s32[64,1,12]{2,1,0:T(1,128)} %bitcast.1), calls=%async_computation | async-start | bytes 65536 | tf_op jit(solution)/shard_map/all_to_all | solution.py:67
  39.2 19.6 %all-to-all-start.2 = ((s32[64,1,12]{2,1,0:T(1,128)}), s32[64,1,12]{2,1,0:T(1,128)S(1)}, u32[]{:S(2)}, u32[]{:S(2)}) async-start(s32[64,1,12]{2,1,0:T(1,128)} %bitcast.6), calls=%async_computation.2 | async-start | bytes 65536 | tf_op jit(solution)/shard_map/all_to_all | solution.py:68
  58.8 58.6 %all-to-all-start.1 = ((f32[64,12,400]{2,1,0:T(8,128)}), f32[64,12,400]{2,1,0:T(8,128)S(1)}, u32[]{:S(2)}, u32[]{:S(2)}) async-start(f32[64,12,400]{2,1,0:T(8,128)} %reshape.203), calls=%async_computation.1 | async-start | bytes 4194304 | tf_op jit(solution)/shard_map/all_to_all | solution.py:71
  76.9 49.7 %copy-start.7 = (s32[384]{0:T(512)S(1)}, s32[384]{0:T(512)}, u32[]{:S(2)}) copy-start(s32[384]{0:T(512)} %param.11) | copy-start | bytes 4612
  117.4 1.3 copy-start.2
  118.8 57.2 %all-to-all-start.3 = ((f32[64,12,400]{2,1,0:T(8,128)}), f32[64,12,400]{2,1,0:T(8,128)}, u32[]{:S(2)}, u32[]{:S(2)}) async-start(f32[64,12,400]{2,1,0:T(8,128)} %reshape.209), calls=%async_computation.3 | async-start | bytes 4194304 | tf_op jit(solution)/shard_map/all_to_all | solution.py:74
  128.3 0.7 copy-start.8
  186.6 7.4 %copy-start.5 = (f32[3,128,400]{1,0,2:T(4,128)S(1)}, f32[3,128,400]{1,0,2:T(4,128)}, u32[]{:S(2)}) copy-start(f32[3,128,400]{1,0,2:T(4,128)} %mul.52) | copy-start | bytes 1843204
  186.6 57.0 %all-to-all-start.4 = ((f32[64,12,400]{2,1,0:T(8,128)}), f32[64,12,400]{2,1,0:T(8,128)}, u32[]{:S(2)}, u32[]{:S(2)}) async-start(f32[64,12,400]{2,1,0:T(8,128)} %reshape.214), calls=%async_computation.4 | async-start | bytes 4194304 | tf_op jit(solution)/shard_map/all_to_all | solution.py:95
  243.6 56.8 %all-to-all-start.5 = ((f32[64,12,400]{2,1,0:T(8,128)}), f32[64,12,400]{2,1,0:T(8,128)}, u32[]{:S(2)}, u32[]{:S(2)}) async-start(f32[64,12,400]{2,1,0:T(8,128)} %reshape.217), calls=%async_computation.5 | async-start | bytes 4194304 | tf_op jit(solution)/shard_map/all_to_all | solution.py:96
  250.8 2.5 copy-start.4
  250.8 216.3 %all-gather.3.cloned.1.call-start = ((), (), s32[]{:S(2)}) async-start(), calls=%async_computation.7 | async-start | bytes 20971520 | tf_op jit(solution)/shard_map/all_gather | solution.py:100
  252.2 2.2 copy-start.3
  253.3 1.1 copy-start.6
  312.7 177.4 %all-reduce.2.cloned.1.call-start = ((), (), s32[]{:S(2)}) async-start(), calls=%async_computation.6 | async-start | bytes 262144 | tf_op jit(solution)/shard_map/psum | solution.py:101
  477.6 14.0 %copy-start.1 = (f32[64,400]{1,0:T(8,128)S(1)}, f32[64,400]{1,0:T(8,128)}, u32[]{:S(2)}) copy-start(f32[64,400]{1,0:T(8,128)} %param.9) | copy-start | bytes 307204
Sparse Core Ops, SparseCore 0:
  312.8 154.2 all-gather.2
Sparse Core Ops, SparseCore 1:
  317.2 172.8 all-reduce.1
